TPU v7x, 32 devices: a whole 2x2x4 slice. The times are simulated.
32 devices in a mesh: doc: 4 (over y, x), label: 8 (over z, core).
Axes of the slice: x: 2, y: 2, z: 4, core: 2. Of those that a mesh axis runs over, the one named last changes fastest.
Arguments:
- doc_embed: bfloat16 [1024, 768], P(('doc', 'label')), may hold values from -0.59765625 to 0.59765625
- classifier: bfloat16 [8192, 768], P('label'), may hold values from -4.28125 to 4.28125
- centroids: bfloat16 [64, 768], P('doc'), may hold values from -4.28125 to 4.28125
- shortlist: int32 [1024, 32], P(('doc', 'label')), may hold values from 0 to 63, all different within a row
- positives: int32 [1024, 4], P(('doc', 'label')), may hold values from 0 to 4095
Outputs:
- grad_classifier: bfloat16 [8192, 768], P('label')
- grad_centroids: float32 [64, 768], P('doc')
- grad_docs: bfloat16 [1024, 768], P(('doc', 'label'))
Inputs may be any that keep to these rules, and one draw needn't show every extreme that they name: `shortlist`: each row names 32 different clusters; every cluster is named by some row.
All inputs are finite; a program needn't handle non-finite values.
Results may differ from a plain program's by a relative error of at most 0.015.
Values may be sent and summed in bfloat16 or wider, within the bound.
A program may use at most 64 MiB of HBM per device.

v0:
```python
import jax
import jax.numpy as jnp
from jax import lax
from jax.sharding import PartitionSpec as P

CLS = 128


LOSS_WEIGHT = 0.125


def tile_grads(rows, short_rows, pos_rows, classifier, cent_rows, cluster_base):
    labels_dev = classifier.shape[0]
    local_clusters = cluster_base + jnp.arange(labels_dev // CLS, dtype=jnp.int32)
    local_labels = cluster_base * CLS + jnp.arange(labels_dev, dtype=jnp.int32)
    logits = jnp.einsum("nd,ld->nl", rows, classifier, preferred_element_type=jnp.float32)
    member = jnp.any(short_rows[:, :, None] == local_clusters[None, None, :], axis=1)
    mask = jnp.repeat(member, CLS, axis=1)
    target = jnp.any(pos_rows[:, :, None] == local_labels[None, None, :], axis=1)
    grad = (
        LOSS_WEIGHT
        * (jax.nn.sigmoid(logits) - target.astype(jnp.float32))
        * mask.astype(jnp.float32)
    ).astype(jnp.bfloat16)
    meta_logits = jnp.einsum("nd,cd->nc", rows, cent_rows, preferred_element_type=jnp.float32)
    pos_clusters = pos_rows // CLS
    meta_target = jnp.any(pos_clusters[:, :, None] == local_clusters[None, None, :], axis=1)
    meta_grad = (
        LOSS_WEIGHT * (jax.nn.sigmoid(meta_logits) - meta_target.astype(jnp.float32))
    ).astype(jnp.bfloat16)
    return (grad, meta_grad)


def body(doc_embed, classifier, centroids, shortlist, positives):
    labels_dev = classifier.shape[0]
    cl_here = labels_dev // CLS
    per_doc = centroids.shape[0]
    label_index = lax.axis_index("label")
    cluster_base = label_index * cl_here
    pos_cluster = jnp.take_along_axis(shortlist, positives // CLS, axis=1)
    pos_label = pos_cluster * CLS + positives % CLS
    all_cent = lax.all_gather(centroids, "doc", axis=0, tiled=True)
    cent_rows = lax.dynamic_slice_in_dim(all_cent, cluster_base, cl_here, 0)
    rows, short_rows, pos_rows = (
        lax.all_gather(doc_embed, "label", axis=0, tiled=True),
        lax.all_gather(shortlist, "label", axis=0, tiled=True),
        lax.all_gather(pos_label, "label", axis=0, tiled=True),
    )
    grad, meta_grad = tile_grads(rows, short_rows, pos_rows, classifier, cent_rows, cluster_base)
    class_acc = jnp.einsum("nl,nd->ld", grad, rows, preferred_element_type=jnp.float32)
    cent_acc = jnp.einsum("nc,nd->cd", meta_grad, rows, preferred_element_type=jnp.float32)
    input_sum = lax.psum_scatter(
        (
            jnp.dot(grad, classifier, preferred_element_type=jnp.float32)
            + jnp.dot(meta_grad, cent_rows, preferred_element_type=jnp.float32)
        ).astype(jnp.bfloat16),
        "label",
        scatter_dimension=0,
        tiled=True,
    )
    grad_classifier = lax.psum(class_acc.astype(jnp.bfloat16), "doc")
    cent_summed = lax.psum(cent_acc, "doc")
    cent_whole = lax.all_gather(cent_summed, "label", axis=0, tiled=True)
    grad_centroids = lax.dynamic_slice_in_dim(
        cent_whole, lax.axis_index("doc") * per_doc, per_doc, 0
    )
    return (grad_classifier, grad_centroids, input_sum)


def solution(mesh):
    in_specs = (
        P(("doc", "label"), None),
        P("label", None),
        P("doc", None),
        P(("doc", "label"), None),
        P(("doc", "label"), None),
    )
    out_specs = (P("label", None), P("doc", None), P(("doc", "label"), None))
    return jax.shard_map(body, mesh=mesh, in_specs=in_specs, out_specs=out_specs, check_vma=False)
```

profile of v0, /device:TPU:0, one launch (start us, length us, event | category | flops | bytes accessed | tf_op | source)
XLA Modules:
  0.0 140.3 jit_solution(11268395638735281398)
XLA Ops:
  8.0 0.0 copy-start
  8.0 0.0 copy-start.1
  8.0 0.0 reduce-scatter.2.cloned.1.call-start
  8.1 0.8 bitcast_or_fusion
  8.9 0.1 copy.47
  9.0 0.1 reshape.31
  9.1 15.9 %all_gather.15 = s32[256,32]{1,0:T(8,128)S(1)} all-gather(s32[32,32]{1,0:T(8,128)} %param.8), channel_id=1, replica_groups=mesh['doc'=4,'label'=8] {'label'}, dimensions={0}, use_global_device_ids=true | all-gather | bytes 36864 | tf_op jit(solution)/shard_map/all_gather | solution.py:46
  25.0 0.0 copy-done.1
  25.0 0.0 copy-start.4
  25.0 0.0 copy-start.3
  25.0 0.0 copy-start.2
  25.0 1.3 gather_fusion
  26.3 0.1 reshape.34
  26.4 0.1 copy.48
  26.5 0.0 copy-done.4
  26.5 12.7 %all-gather = s32[8,32,4]{1,2,0:T(4,128)S(1)} all-gather(s32[1,32,4]{1,2,0:T(4,128)S(1)} %fusion.20), channel_id=1, replica_groups=mesh['doc'=4,'label'=8] {'label'}, dimensions={0}, use_global_device_ids=true | all-gather | bytes 4608 | tf_op jit(solution)/shard_map/all_gather | solution.py:47
  39.2 0.1 reshape.43
  39.3 0.0 copy-done.3
  39.3 8.4 %all_gather.18 = bf16[64,768]{1,0:T(8,128)(2,1)S(1)} all-gather(bf16[16,768]{1,0:T(8,128)(2,1)S(1)} %copy-done.3), channel_id=1, replica_groups=mesh['doc'=4,'label'=8] {'doc'}, dimensions={0}, use_global_device_ids=true | all-gather | bytes 122880 | tf_op jit(solution)/shard_map/all_gather | solution.py:42
  47.7 0.1 copy.45
  47.8 0.1 compare_reduce_fusion.2
  47.9 0.1 compare_reduce_fusion.1
  48.0 0.2 copy.46
  48.1 0.6 compare_reduce_fusion
  48.7 0.0 copy-done.2
  48.7 14.6 %all_gather.16 = bf16[256,768]{1,0:T(8,128)(2,1)S(1)} all-gather(bf16[32,768]{1,0:T(8,128)(2,1)S(1)} %copy-done.2), channel_id=1, replica_groups=mesh['doc'=4,'label'=8] {'label'}, dimensions={0}, use_global_device_ids=true | all-gather | bytes 442368 | tf_op jit(solution)/shard_map/all_gather | solution.py:45
  63.3 0.3 broadcast_in_dim.6
  63.6 0.0 copy-done
  63.6 0.8 fusion.7
  64.4 0.6 fusion.25
  65.0 0.3 fusion.14
  65.3 1.1 fusion.5
  66.3 0.0 reduce-scatter.2.cloned.1.call-update
  66.4 0.0 all-reduce.2.cloned.1.call-start
  66.4 1.8 %convolution_convert_fusion = bf16[1024,768]{1,0:T(8,128)(2,1)} fusion(bf16[256,1024]{1,0:T(8,128)(2,1)S(1)} %fusion.7, bf16[256,768]{1,0:T(8,128)(2,1)S(1)} %all_gather.16), kind=kOutput, calls=%fused_computation.2 | convolution fusion | flops 403439616 | bytes 2490368 | tf_op jit(solution)/shard_map/nl,nd->ld/dot_general | solution.py:50
  68.2 0.0 all-reduce.2.cloned.1.call-update
  68.2 0.2 fusion.24
  68.4 15.9 %psum.15 = f32[8,768]{1,0:T(8,128)S(1)} all-reduce(f32[8,768]{1,0:T(8,128)S(1)} %fusion.24), channel_id=1, replica_groups=mesh['doc'=4,'label'=8] {'doc'}, use_global_device_ids=true, to_apply=%region_4.5 | all-reduce | flops 6144 | bytes 49152 | tf_op jit(solution)/shard_map/psum | solution.py:62
  84.3 14.1 %all_gather.19 = f32[64,768]{1,0:T(8,128)S(1)} all-gather(f32[8,768]{1,0:T(8,128)S(1)} %psum.15), channel_id=1, replica_groups=mesh['doc'=4,'label'=8] {'label'}, dimensions={0}, use_global_device_ids=true | all-gather | bytes 221184 | tf_op jit(solution)/shard_map/all_gather | solution.py:63
  98.5 0.6 constant_dynamic-slice_fusion
  99.1 0.0 reduce-scatter.2.cloned.1.call-done
  99.1 31.1 %all-reduce.2.cloned.1.call-done = bf16[1024,768]{1,0:T(8,128)(2,1)} async-done(((bf16[1024,768]{1,0:T(8,128)(2,1)}), bf16[1024,768]{1,0:T(8,128)(2,1)}) %all-reduce.2.cloned.1.call-update) | async-done | bytes 1572880 | tf_op jit(solution)/shard_map/psum | solution.py:61
  130.2 2.7 %copy.53 = bf16[1024,768]{1,0:T(8,128)(2,1)} copy(bf16[1024,768]{1,0:T(8,128)(2,1)} %all-reduce.2.cloned.1.call-done) | data formatting | bytes 3145728
  (5 shorter events, 0.0 us)
Async XLA Ops:
  8.0 55.6 %copy-start = (bf16[1024,768]{1,0:T(8,128)(2,1)S(1)}, bf16[1024,768]{1,0:T(8,128)(2,1)}, u32[]{:S(2)}) copy-start(bf16[1024,768]{1,0:T(8,128)(2,1)} %param.6) | copy-start | bytes 4718596
  8.0 17.0 %copy-start.1 = (s32[32,32]{1,0:T(8,128)S(1)}, s32[32,32]{1,0:T(8,128)}, u32[]{:S(2)}) copy-start(s32[32,32]{1,0:T(8,128)} %param.8) | copy-start | bytes 12292
  8.0 91.1 %reduce-scatter.2.cloned.1.call-start = ((), (), s32[]{:S(2)}) async-start(), calls=%async_computation.2 | async-start | bytes 442368 | tf_op jit(solution)/shard_map/reduce_scatter | solution.py:52
  25.0 1.5 %copy-start.4 = (s32[32,4]{0,1:T(4,128)S(1)}, s32[32,4]{0,1:T(4,128)}, u32[]{:S(2)}) copy-start(s32[32,4]{0,1:T(4,128)} %param.9) | copy-start | bytes 1540
  25.0 14.3 %copy-start.3 = (bf16[16,768]{1,0:T(8,128)(2,1)S(1)}, bf16[16,768]{1,0:T(8,128)(2,1)}, u32[]{:S(2)}) copy-start(bf16[16,768]{1,0:T(8,128)(2,1)} %param.7) | copy-start | bytes 73732
  25.0 23.7 %copy-start.2 = (bf16[32,768]{1,0:T(8,128)(2,1)S(1)}, bf16[32,768]{1,0:T(8,128)(2,1)}, u32[]{:S(2)}) copy-start(bf16[32,768]{1,0:T(8,128)(2,1)} %param.5) | copy-start | bytes 147460
  66.4 63.8 %all-reduce.2.cloned.1.call-start = ((), (), s32[]{:S(2)}) async-start(), calls=%async_computation.1 | async-start | bytes 3145728 | tf_op jit(solution)/shard_map/psum | solution.py:61
Sparse Core Ops, SparseCore 0:
  66.5 29.4 reduce-scatter.1
Sparse Core Ops, SparseCore 1:
  70.5 59.6 all-reduce.1
where the time goes:
time: 141 us; the launch traced here: 140 us
  blocking collectives  81.6 us (58%)
  waiting for transfers between devices  31.1 us (22%)
  between operations  15.6 us (11%)
  local copies, waits for them, and re-layouts  5.58 us (4%)
  matrix products  4.62 us (3%)
  other arithmetic  1.61 us (1%)
    psum x1, waiting for transfers between devices, body(): grad_classifier = lax.psum(class_acc.astype(jnp.bfloat16), 'doc')  31.1 us
    psum x1, blocking collectives, body(): cent_summed = lax.psum(cent_acc, 'doc')  15.9 us
    all_gather x1, blocking collectives, body(): lax.all_gather(shortlist, 'label', axis=0, tiled=True)  15.9 us
    all_gather x1, blocking collectives, body(): lax.all_gather(doc_embed, 'label', axis=0, tiled=True)  14.6 us
    all_gather x1, blocking collectives, body(): cent_whole = lax.all_gather(cent_summed, 'label', axis=0, tiled=True)  14.1 us
    all_gather x1, blocking collectives, body(): lax.all_gather(pos_label, 'label', axis=0, tiled=True)  12.7 us
    all_gather x1, blocking collectives, body(): all_cent = lax.all_gather(centroids, 'doc', axis=0, tiled=True)  8.37 us
  transfers between devices with their start and end apart: 2, of which 1 were waited for; matrix products, arithmetic and copies ran while one was open for 2% of the time, Pallas kernels for 0%

commit v1 on v0

v1 whole, which is shorter than its diff:
```python
import functools

import jax
import jax.numpy as jnp
from jax import lax
from jax.experimental import pallas as pl
from jax.experimental.pallas import tpu as pltpu
from jax.sharding import PartitionSpec as P

CLS = 128
INFO = 128
TILE = 256
EIGHTH = 0.125
F32 = jnp.float32
BF16 = jnp.bfloat16
MESH = pl.DeviceIdType.MESH
NT = (((1,), (1,)), ((), ()))
TN = (((0,), (0,)), ((), ()))


def flip(a, k, n):
    out, bit = 0, 1
    while bit < n:
        b = lax.rem(lax.div(a, bit), 2)
        out = out + bit * ((1 - b) if (k // bit) % 2 else b)
        bit *= 2
    return out


def sigmoid_grad(logits, target):
    return (EIGHTH / 2) * jnp.tanh(0.5 * logits) + jnp.where(target, -EIGHTH / 2, EIGHTH / 2)


def kernel(
    n_doc, n_label, pos_n,
    doc_ref, cls_hbm, cent_ref, short_ref, pos_ref,
    gcls_ref, gcent_ref, gdoc_ref,
    docs, cls, info_t, acc, part, cent_in, pair_out, pair_in, tot, rs_out, rs_in,
    cls_sem, sib_send, z_send, g_send, cent_send, pair_send, rs_send,
    recv, cent_recv, pair_recv, rs_recv,
):
    rows, width = doc_ref.shape
    labels = cls.shape[0]
    here = labels // CLS
    per = cent_ref.shape[0]
    n_z = n_label // 2
    group = n_label * rows
    d = lax.axis_index("doc")
    l = lax.axis_index("label")
    z, c = lax.div(l, 2), lax.rem(l, 2)
    sib = z * 2 + (1 - c)

    load = pltpu.make_async_copy(cls_hbm, cls, cls_sem)
    load.start()

    barrier = pltpu.get_barrier_semaphore()
    peers = [(d, sib)]
    peers += [(d, flip(z, k, n_z) * 2 + c) for k in range(1, n_z)]
    peers += [(flip(d, k, n_doc), l) for k in range(1, n_doc)]
    for peer in peers:
        pl.semaphore_signal(barrier, inc=1, device_id=peer, device_id_type=MESH)

    own = c * n_z + z
    docs[d, own, :, 0:width] = doc_ref[...]
    short = short_ref[...]
    slots = short.shape[1]
    lane = lax.broadcasted_iota(jnp.int32, (rows, INFO), 1)
    short_wide = jnp.concatenate([short, jnp.zeros((rows, INFO - slots), jnp.int32)], axis=1)
    wide = short_wide
    for p in range(pos_n):
        at = pos_ref[:, p : p + 1]
        slot = lax.div(at, CLS)
        cluster = jnp.sum(jnp.where(lane == slot, short_wide, 0), axis=1, keepdims=True)
        wide = jnp.where(lane == slots + p, cluster, wide)
        wide = jnp.where(lane == slots + pos_n + p, lax.rem(at, CLS), wide)
    docs[d, own, :, width:] = wide.astype(F32).astype(BF16)

    pl.semaphore_wait(barrier, len(peers))

    sends = []

    def send(ref, sem, rsem, peer):
        copy = pltpu.make_async_remote_copy(
            src_ref=ref, dst_ref=ref, send_sem=sem, recv_sem=rsem, device_id=peer, device_id_type=MESH
        )
        copy.start()
        sends.append(copy)

    def arrive(ref, rsem):
        pltpu.make_async_remote_copy(
            src_ref=ref, dst_ref=ref, send_sem=cls_sem, recv_sem=rsem, device_id=(d, sib), device_id_type=MESH
        ).wait_recv()

    def slot_send(g, s, sem, peer):
        send(docs.at[g, s], sem, recv.at[g, s], peer)

    def slot_arrive(g, s):
        arrive(docs.at[g, s], recv.at[g, s])

    def same(k):
        return c * n_z + flip(z, k, n_z)

    def other(k):
        return (1 - c) * n_z + flip(z, k, n_z)

    owner = lax.div(l * here, per)
    for k in range(1, n_doc):
        to = flip(d, k, n_doc)
        copy = pltpu.make_async_remote_copy(
            src_ref=cent_ref, dst_ref=cent_in, send_sem=cent_send.at[k], recv_sem=cent_recv,
            device_id=(to, l), device_id_type=MESH,
        )

        @pl.when(d == owner)
        def _():
            copy.start()

    @pl.when(d == owner)
    def _():
        cent_in[...] = cent_ref[...]

    for k in range(n_z - 1, 0, -1):
        slot_send(d, own, z_send.at[k], (d, flip(z, k, n_z) * 2 + c))

    ring = n_doc == 4
    nears = (1, 2) if ring else tuple(range(1, n_doc))
    g_pass = flip(d, 1, n_doc) * (1 - c) + flip(d, 2, n_doc) * c
    g_keep = flip(d, 2, n_doc) * (1 - c) + flip(d, 1, n_doc) * c

    def spread(k):
        for i in nears:
            slot_send(d, same(k), g_send.at[i, k], (flip(d, i, n_doc), l))
        slot_send(d, same(k), sib_send.at[0, k], (d, sib))

    def relay(k):
        if ring:
            slot_arrive(g_pass, same(k))
            slot_send(g_pass, same(k), g_send.at[3, k], (g_keep, l))
            slot_send(g_pass, same(k), sib_send.at[1, k], (d, sib))
            slot_arrive(g_keep, same(k))
            slot_send(g_keep, same(k), sib_send.at[2, k], (d, sib))
        else:
            for i in nears:
                g = flip(d, i, n_doc)
                slot_arrive(g, same(k))
                slot_send(g, same(k), sib_send.at[i, k], (d, sib))

    ready = [d]
    for k in range(n_z):
        if k:
            slot_arrive(d, same(k))
        spread(k)
        if k:
            relay(k - 1)

    load.wait()

    def rows_of(g):
        return docs[g].reshape(group, width + INFO)

    def work(g, first, last):
        info_t[...] = rows_of(g)[:, width:].astype(F32).T
        if first:
            part[...] = jnp.zeros_like(part)

        def tile(t, carry):
            at = pl.ds(pl.multiple_of(t * TILE, TILE), TILE)
            x = rows_of(g)[:, :width]
            w = cls[at, :]
            logits = lax.dot_general(w, x, NT, preferred_element_type=F32)
            label = lax.broadcasted_iota(jnp.int32, (CLS, group), 0).astype(F32)
            pieces = []
            for j in range(TILE // CLS):
                cid = (l * here + t * (TILE // CLS) + j).astype(F32)
                member = jnp.max(jnp.where(info_t[0:slots, :] == cid, 1.0, 0.0), axis=0, keepdims=True)
                hit = None
                for p in range(pos_n):
                    pc = info_t[slots + p : slots + p + 1, :]
                    pw = info_t[slots + pos_n + p : slots + pos_n + p + 1, :]
                    this = label == jnp.where(pc == cid, pw, -1.0)
                    hit = this if hit is None else hit | this
                grad = sigmoid_grad(logits[j * CLS : (j + 1) * CLS, :], hit) * member
                pieces.append(grad.astype(BF16))
            grad = jnp.concatenate(pieces, axis=0)
            total = jnp.dot(grad, x, preferred_element_type=F32)
            if not first:
                total = total + acc[at, :]
            if last:
                gcls_ref[at, :] = total.astype(BF16)
            else:
                acc[at, :] = total
            if first:
                part[...] += lax.dot_general(grad, w, TN, preferred_element_type=F32)
            return carry

        lax.fori_loop(0, labels // TILE, tile, 0)

        def meta(cents, base):
            x = rows_of(g)[:, :width]
            logits = lax.dot_general(cents, x, NT, preferred_element_type=F32)
            cid = (lax.broadcasted_iota(jnp.int32, (per, group), 0) + base).astype(F32)
            hit = None
            for p in range(pos_n):
                this = cid == info_t[slots + p : slots + p + 1, :]
                hit = this if hit is None else hit | this
            return sigmoid_grad(logits, hit), cid

        mine, _ = meta(cent_ref[...], d * per)
        total = jnp.dot(mine.astype(BF16), rows_of(g)[:, :width], preferred_element_type=F32)
        gcent_ref[...] = total if first else gcent_ref[...] + total
        if first:
            @pl.when(d != owner)
            def _():
                arrive(cent_in, cent_recv)

            base = owner * per
            some, cid = meta(cent_in[...], base)
            low = (l * here).astype(F32)
            some = jnp.where((cid >= low) & (cid < low + here), some, 0.0).astype(BF16)
            part[...] += lax.dot_general(some, cent_in[...], TN, preferred_element_type=F32)

    for k in range(n_z):
        slot_arrive(d, other(k))
    work(d, True, n_doc == 1)

    half = group // 2
    pair_out[...] = part[pl.ds(pl.multiple_of((1 - c) * half, half), half), :].astype(BF16)
    pair = pltpu.make_async_remote_copy(
        src_ref=pair_out, dst_ref=pair_in, send_sem=pair_send, recv_sem=pair_recv,
        device_id=(d, sib), device_id_type=MESH,
    )
    pair.start()
    sends.append(pair)
    relay(n_z - 1)
    pair.wait_recv()
    tot[...] = part[pl.ds(pl.multiple_of(c * half, half), half), :] + pair_in[...].astype(F32)
    rs_out[...] = tot[...].astype(BF16).reshape(n_z, rows, width)
    for k in range(n_z - 1, 0, -1):
        to = flip(z, k, n_z)
        copy = pltpu.make_async_remote_copy(
            src_ref=rs_out.at[to], dst_ref=rs_in.at[z], send_sem=rs_send.at[k], recv_sem=rs_recv.at[z],
            device_id=(d, to * 2 + c), device_id_type=MESH,
        )
        copy.start()
        sends.append(copy)

    for i in range(1, n_doc):
        if ring:
            g = (None, g_pass, g_keep, flip(d, 3, n_doc))[i]
        else:
            g = flip(d, i, n_doc)
        for k in range(n_z):
            if ring and i == 3:
                slot_arrive(g, same(k))
                slot_send(g, same(k), sib_send.at[3, k], (d, sib))
        for k in range(n_z):
            slot_arrive(g, other(k))
        work(g, False, i == n_doc - 1)

    out = tot[pl.ds(pl.multiple_of(z * rows, rows), rows), :]
    for k in range(1, n_z):
        src = flip(z, k, n_z)
        arrive(rs_in.at[src], rs_recv.at[src])
        out = out + rs_in[src].astype(F32)
    gdoc_ref[...] = out.astype(BF16)

    for copy in sends:
        copy.wait_send()
    for k in range(1, n_doc):
        @pl.when(d == owner)
        def _():
            pltpu.make_async_remote_copy(
                src_ref=cent_ref, dst_ref=cent_in, send_sem=cent_send.at[k], recv_sem=cent_recv,
                device_id=(d, sib), device_id_type=MESH,
            ).wait_send()


def solution(mesh):
    n_doc, n_label = mesh.shape["doc"], mesh.shape["label"]
    n_z = n_label // 2

    def body(doc_embed, classifier, centroids, shortlist, positives):
        rows, width = doc_embed.shape
        labels = classifier.shape[0]
        per = centroids.shape[0]
        group = n_label * rows
        vmem = pl.BlockSpec(memory_space=pltpu.VMEM)
        dma = pltpu.SemaphoreType.DMA
        return pl.pallas_call(
            functools.partial(kernel, n_doc, n_label, positives.shape[1]),
            out_shape=(
                jax.ShapeDtypeStruct((labels, width), BF16),
                jax.ShapeDtypeStruct((per, width), F32),
                jax.ShapeDtypeStruct((rows, width), BF16),
            ),
            in_specs=[vmem, pl.BlockSpec(memory_space=pl.ANY), vmem, vmem, vmem],
            out_specs=(vmem, vmem, vmem),
            scratch_shapes=[
                pltpu.VMEM((n_doc, n_label, rows, width + INFO), BF16),
                pltpu.VMEM((labels, width), BF16),
                pltpu.VMEM((INFO, group), F32),
                pltpu.VMEM((labels, width), F32),
                pltpu.VMEM((group, width), F32),
                pltpu.VMEM((per, width), BF16),
                pltpu.VMEM((group // 2, width), BF16),
                pltpu.VMEM((group // 2, width), BF16),
                pltpu.VMEM((group // 2, width), F32),
                pltpu.VMEM((n_z, rows, width), BF16),
                pltpu.VMEM((n_z, rows, width), BF16),
                dma(()),
                dma((n_doc, n_z)),
                dma((n_z,)),
                dma((n_doc, n_z)),
                dma((n_doc,)),
                dma(()),
                dma((n_z,)),
                dma((n_doc, n_label)),
                dma(()),
                dma(()),
                dma((n_z,)),
            ],
            compiler_params=pltpu.CompilerParams(
                collective_id=0, has_side_effects=True, vmem_limit_bytes=60 * 1024 * 1024
            ),
        )(doc_embed, classifier, centroids, shortlist, positives)

    in_specs = (
        P(("doc", "label"), None),
        P("label", None),
        P("doc", None),
        P(("doc", "label"), None),
        P(("doc", "label"), None),
    )
    out_specs = (P("label", None), P("doc", None), P(("doc", "label"), None))
    return jax.shard_map(body, mesh=mesh, in_specs=in_specs, out_specs=out_specs, check_vma=False)
```

time: 141 us -> 40.4 us (0.29)
  blocking collectives: 81.6 us -> 0 us
  Pallas kernels: 0 us -> 34.2 us
  waiting for transfers between devices: 31.1 us -> 0 us
  between operations: 15.6 us -> 0.66 us
  matrix products: 4.62 us -> 0 us
  other arithmetic: 1.61 us -> 0 us
    all_gather x5 -> x0, blocking collectives: 65.7 us -> none  [the longest x1 15.9 us: body(): lax.all_gather(shortlist, 'label', axis=0, tiled=True)]
    pallas_call x0 -> x1, Pallas kernels: none -> 34.2 us  [body(): pl.pallas_call(functools.partial(kernel, n_doc, n_label, positives.shape[...]
    psum x1 -> x0, waiting for transfers between devices: 31.1 us -> none  [body(): grad_classifier = lax.psum(class_acc.astype(jnp.bfloat16), 'doc')]
    psum x1 -> x0, blocking collectives: 15.9 us -> none  [body(): cent_summed = lax.psum(cent_acc, 'doc')]
    dot_general x6 -> x0, matrix products: 4.62 us -> none  [the longest x1 1.77 us: body(): jnp.einsum('nl,nd->ld', grad, rows, preferred_element_type=jnp.float32)]
    unnamed x12 -> x8, local copies, waits for them, and re-layouts: 2.76 us -> 5.29 us
    gather x5 -> x0, local copies, waits for them, and re-layouts: 1.63 us -> none  [body(): pos_cluster = jnp.take_along_axis(shortlist, positives // CLS, axis=1)]
  transfers between devices with their start and end apart: 2 -> 0, of which waited for: 1 -> 0; matrix products, arithmetic and copies ran while one was open for 2% -> 0% of each run, Pallas kernels for 0% -> 0%
where the time goes in v1:
time: 40.4 us; the launch traced here: 40.2 us
  Pallas kernels  34.2 us (85%)
  local copies, waits for them, and re-layouts  5.29 us (13%)
  between operations  0.66 us (2%)
    pallas_call x1, Pallas kernels, body(): pl.pallas_call(functools.partial(kernel, n_doc, n_label, positives.shape[...  34.2 us
    unnamed x8, local copies, waits for them, and re-layouts  5.29 us

profile of v1, /device:TPU:0, one launch (start us, length us, event | category | flops | bytes accessed | tf_op | source)
XLA Modules:
  0.0 40.2 jit_solution(156749053378127673)
XLA Ops:
  0.6 1.4 %copy.8.pos_ref = s32[32,4]{1,0:T(8,128)} copy(s32[32,4]{0,1:T(4,128)} %param.9) | data formatting | bytes 1024 | tf_op args[4]
  2.0 34.2 %shard_map.76 = (bf16[1024,768]{1,0:T(8,128)(2,1)}, f32[16,768]{1,0:T(8,128)}, bf16[32,768]{1,0:T(8,128)(2,1)}) custom-call(bf16[32,768]{1,0:T(8,128)(2,1)} %doc_ref.1, bf16[1024,768]{1,0:T(8,128)(2,1)} %cls_hbm.1, bf16[16,768]{1,0:T(8,128)(2,1)} %cent_ref.1, s32[32,32]{1,0:T(8,128)} %short_ref.1, s32[32,4]{1,0:T(8,128)} %copy.8.pos_ref), custom_call_target="tpu_custom_call" | custom-call | tf_op jit(solution)/shard_map/pallas_call | solution.py:289
  36.2 0.0 copy-start.1
  36.2 0.0 copy-start
  36.2 2.7 %copy.12 = bf16[1024,768]{1,0:T(8,128)(2,1)} copy(bf16[1024,768]{1,0:T(8,128)(2,1)} %get-tuple-element.6) | data formatting | bytes 3145728
  38.9 0.0 copy-done.1
  38.9 0.6 %copy.13 = f32[16,768]{1,0:T(8,128)} copy(f32[16,768]{1,0:T(8,128)S(1)} %copy-done.1) | data formatting | bytes 98304
  39.5 0.0 copy-done
  39.5 0.6 %copy.14 = bf16[32,768]{1,0:T(8,128)(2,1)} copy(bf16[32,768]{1,0:T(8,128)(2,1)S(1)} %copy-done) | data formatting | bytes 98304
Async XLA Ops:
  36.2 2.7 %copy-start.1 = (f32[16,768]{1,0:T(8,128)S(1)}, f32[16,768]{1,0:T(8,128)}, u32[]{:S(2)}) copy-start(f32[16,768]{1,0:T(8,128)} %get-tuple-element.7) | copy-start | bytes 147460
  36.2 3.3 %copy-start = (bf16[32,768]{1,0:T(8,128)(2,1)S(1)}, bf16[32,768]{1,0:T(8,128)(2,1)}, u32[]{:S(2)}) copy-start(bf16[32,768]{1,0:T(8,128)(2,1)} %get-tuple-element.8) | copy-start | bytes 147460

commit v2 on v1

v2 whole, which is shorter than its diff:
```python
import functools

import jax
import jax.numpy as jnp
from jax import lax
from jax.experimental import pallas as pl
from jax.experimental.pallas import tpu as pltpu
from jax.sharding import PartitionSpec as P

CLS = 128
INFO = 128
EIGHTH = 0.125
F32 = jnp.float32
BF16 = jnp.bfloat16
MESH = pl.DeviceIdType.MESH
NT = (((1,), (1,)), ((), ()))
TN = (((0,), (0,)), ((), ()))


def flip(a, k, n):
    out, bit = 0, 1
    while bit < n:
        b = lax.rem(lax.div(a, bit), 2)
        out = out + bit * ((1 - b) if (k // bit) % 2 else b)
        bit *= 2
    return out


def sigmoid_grad(logits, target):
    return (EIGHTH / 2) * jnp.tanh(0.5 * logits) + jnp.where(target, -EIGHTH / 2, EIGHTH / 2)


def kernel(
    n_doc, n_label, pos_n,
    doc_ref, cls_hbm, cent_ref, short_ref, pos_ref,
    gcls_ref, gcent_ref, gdoc_ref,
    docs, cls, info_t, acc, part, cent_in, pair_out, pair_in, tot, rs_out, rs_in,
    cls_sem, sib_send, z_send, g_send, cent_send, pair_send, rs_send,
    sib_recv, z_recv, g_recv, cent_recv, pair_recv, rs_recv,
):
    rows, width = doc_ref.shape
    labels = cls.shape[0]
    here = labels // CLS
    per = cent_ref.shape[0]
    n_z = n_label // 2
    group = n_label * rows
    step = min(labels, max(2 * CLS, (1 << 18) // group))
    d = lax.axis_index("doc")
    l = lax.axis_index("label")
    z, c = lax.div(l, 2), lax.rem(l, 2)
    sib = z * 2 + (1 - c)

    load = pltpu.make_async_copy(cls_hbm, cls, cls_sem)
    load.start()

    barrier = pltpu.get_barrier_semaphore()
    peers = [(d, sib)]
    peers += [(d, flip(z, k, n_z) * 2 + c) for k in range(1, n_z)]
    peers += [(flip(d, k, n_doc), l) for k in range(1, n_doc)]
    for peer in peers:
        pl.semaphore_signal(barrier, inc=1, device_id=peer, device_id_type=MESH)

    docs[0, 0, 0, :, 0:width] = doc_ref[...]
    short = short_ref[...]
    slots = short.shape[1]
    lane = lax.broadcasted_iota(jnp.int32, (rows, INFO), 1)
    short_wide = jnp.concatenate([short, jnp.zeros((rows, INFO - slots), jnp.int32)], axis=1)
    pos_t = pos_ref[...].T
    wide = short_wide
    for p in range(pos_n):
        at = pos_t[:, p : p + 1]
        slot = lax.div(at, CLS)
        cluster = jnp.sum(jnp.where(lane == slot, short_wide, 0), axis=1, keepdims=True)
        wide = jnp.where(lane == slots + p, cluster, wide)
        wide = jnp.where(lane == slots + pos_n + p, lax.rem(at, CLS), wide)
    docs[0, 0, 0, :, width:] = wide.astype(F32).astype(BF16)

    pl.semaphore_wait(barrier, len(peers))

    sends = []

    def send(src, dst, sem, rsem, peer):
        copy = pltpu.make_async_remote_copy(
            src_ref=src, dst_ref=dst, send_sem=sem, recv_sem=rsem, device_id=peer, device_id_type=MESH
        )
        copy.start()
        sends.append(copy)

    def arrive(ref, rsem):
        pltpu.make_async_remote_copy(
            src_ref=ref, dst_ref=ref, send_sem=cls_sem, recv_sem=rsem, device_id=(d, sib), device_id_type=MESH
        ).wait_recv()

    parts = (pl.ds(0, 1), pl.ds(1, n_z - 1))

    def across(h):
        for i in range(1, n_doc):
            send(docs.at[0, 0, parts[h]], docs.at[i, 0, parts[h]], g_send.at[i, h], g_recv.at[i, h], (flip(d, i, n_doc), l))

    def to_sibling(i):
        send(docs.at[i, 0], docs.at[i, 1], sib_send.at[i], sib_recv.at[i], (d, sib))

    owner = lax.div(l * here, per)
    for k in range(1, n_doc):
        to = flip(d, k, n_doc)
        copy = pltpu.make_async_remote_copy(
            src_ref=cent_ref, dst_ref=cent_in, send_sem=cent_send.at[k], recv_sem=cent_recv,
            device_id=(to, l), device_id_type=MESH,
        )

        @pl.when(d == owner)
        def _():
            copy.start()

    @pl.when(d == owner)
    def _():
        cent_in[...] = cent_ref[...]

    for k in range(n_z - 1, 0, -1):
        send(docs.at[0, 0, 0], docs.at[0, 0, k], z_send.at[k], z_recv.at[k], (d, flip(z, k, n_z) * 2 + c))
    across(0)
    for k in range(1, n_z):
        arrive(docs.at[0, 0, k], z_recv.at[k])
    to_sibling(0)
    across(1)

    load.wait()

    def rows_of(g):
        return docs[g].reshape(group, width + INFO)

    def work(g, first, last):
        info_t[...] = rows_of(g)[:, width:].astype(F32).T
        if first:
            part[...] = jnp.zeros_like(part)

        def tile(t, carry):
            at = pl.ds(pl.multiple_of(t * step, step), step)
            x = rows_of(g)[:, :width]
            w = cls[at, :]
            logits = lax.dot_general(w, x, NT, preferred_element_type=F32)
            label = lax.broadcasted_iota(jnp.int32, (CLS, group), 0).astype(F32)
            pieces = []
            for j in range(step // CLS):
                cid = (l * here + t * (step // CLS) + j).astype(F32)
                member = jnp.max(jnp.where(info_t[0:slots, :] == cid, 1.0, 0.0), axis=0, keepdims=True)
                hit = None
                for p in range(pos_n):
                    pc = info_t[slots + p : slots + p + 1, :]
                    pw = info_t[slots + pos_n + p : slots + pos_n + p + 1, :]
                    this = label == jnp.where(pc == cid, pw, -1.0)
                    hit = this if hit is None else hit | this
                grad = sigmoid_grad(logits[j * CLS : (j + 1) * CLS, :], hit) * member
                pieces.append(grad.astype(BF16))
            grad = jnp.concatenate(pieces, axis=0)
            total = jnp.dot(grad, x, preferred_element_type=F32)
            if not first:
                total = total + acc[at, :]
            if last:
                gcls_ref[at, :] = total.astype(BF16)
            else:
                acc[at, :] = total
            if first:
                part[...] += lax.dot_general(grad, w, TN, preferred_element_type=F32)
            return carry

        lax.fori_loop(0, labels // step, tile, 0)

        def meta(cents, base):
            x = rows_of(g)[:, :width]
            logits = lax.dot_general(cents, x, NT, preferred_element_type=F32)
            cid = (lax.broadcasted_iota(jnp.int32, (per, group), 0) + base).astype(F32)
            hit = None
            for p in range(pos_n):
                this = cid == info_t[slots + p : slots + p + 1, :]
                hit = this if hit is None else hit | this
            return sigmoid_grad(logits, hit), cid

        mine, _ = meta(cent_ref[...], d * per)
        total = jnp.dot(mine.astype(BF16), rows_of(g)[:, :width], preferred_element_type=F32)
        gcent_ref[...] = total if first else gcent_ref[...] + total
        if first:
            @pl.when(d != owner)
            def _():
                arrive(cent_in, cent_recv)

            base = owner * per
            some, cid = meta(cent_in[...], base)
            low = (l * here).astype(F32)
            some = jnp.where((cid >= low) & (cid < low + here), some, 0.0).astype(BF16)
            part[...] += lax.dot_general(some, cent_in[...], TN, preferred_element_type=F32)

    arrive(docs.at[0, 1], sib_recv.at[0])
    work(0, True, n_doc == 1)

    half = group // 2
    pair_out[...] = part[half:, :].astype(BF16)
    send(pair_out, pair_in, pair_send, pair_recv, (d, sib))
    for i in range(1, n_doc):
        for h in range(2):
            arrive(docs.at[i, 0, parts[h]], g_recv.at[i, h])
        to_sibling(i)
    arrive(pair_in, pair_recv)
    tot[...] = part[:half, :] + pair_in[...].astype(F32)
    rs_out[...] = tot[...].astype(BF16).reshape(n_z, rows, width)
    for k in range(n_z - 1, 0, -1):
        send(rs_out.at[k], rs_in.at[k], rs_send.at[k], rs_recv.at[k], (d, flip(z, k, n_z) * 2 + c))

    for i in range(1, n_doc):
        arrive(docs.at[i, 1], sib_recv.at[i])
        work(i, False, i == n_doc - 1)

    out = tot[0:rows, :]
    for k in range(1, n_z):
        arrive(rs_in.at[k], rs_recv.at[k])
        out = out + rs_in[k].astype(F32)
    gdoc_ref[...] = out.astype(BF16)

    for copy in sends:
        copy.wait_send()
    for k in range(1, n_doc):
        @pl.when(d == owner)
        def _():
            pltpu.make_async_remote_copy(
                src_ref=cent_ref, dst_ref=cent_in, send_sem=cent_send.at[k], recv_sem=cent_recv,
                device_id=(d, sib), device_id_type=MESH,
            ).wait_send()


def settle_kernel(n, *refs):
    copies = [pltpu.make_async_copy(refs[i], refs[n + i], refs[2 * n].at[i]) for i in range(n)]
    for copy in copies:
        copy.start()
    for copy in copies:
        copy.wait()


def settle(*arrays):
    n = len(arrays)
    return pl.pallas_call(
        functools.partial(settle_kernel, n),
        out_shape=tuple(jax.ShapeDtypeStruct(a.shape, a.dtype) for a in arrays),
        in_specs=[pl.BlockSpec(memory_space=pl.ANY)] * n,
        out_specs=(pl.BlockSpec(memory_space=pl.ANY),) * n,
        scratch_shapes=[pltpu.SemaphoreType.DMA((n,))],
        compiler_params=pltpu.CompilerParams(vmem_limit_bytes=1 << 20),
    )(*arrays)


def solution(mesh):
    n_doc, n_label = mesh.shape["doc"], mesh.shape["label"]
    n_z = n_label // 2

    def body(doc_embed, classifier, centroids, shortlist, positives):
        rows, width = doc_embed.shape
        labels = classifier.shape[0]
        per = centroids.shape[0]
        group = n_label * rows
        vmem = pl.BlockSpec(memory_space=pltpu.VMEM)
        limit = (64 << 20) - (labels * width * 2 + per * width * 4 + rows * width * 2) - (128 << 10)
        dma = pltpu.SemaphoreType.DMA
        outs = pl.pallas_call(
            functools.partial(kernel, n_doc, n_label, positives.shape[1]),
            out_shape=(
                pltpu.VMEM((labels, width), BF16),
                pltpu.VMEM((per, width), F32),
                pltpu.VMEM((rows, width), BF16),
            ),
            in_specs=[vmem, pl.BlockSpec(memory_space=pl.ANY), vmem, vmem, vmem],
            out_specs=(vmem, vmem, vmem),
            scratch_shapes=[
                pltpu.VMEM((n_doc, 2, n_z, rows, width + INFO), BF16),
                pltpu.VMEM((labels, width), BF16),
                pltpu.VMEM((INFO, group), F32),
                pltpu.VMEM((labels, width), F32),
                pltpu.VMEM((group, width), F32),
                pltpu.VMEM((per, width), BF16),
                pltpu.VMEM((group // 2, width), BF16),
                pltpu.VMEM((group // 2, width), BF16),
                pltpu.VMEM((group // 2, width), F32),
                pltpu.VMEM((n_z, rows, width), BF16),
                pltpu.VMEM((n_z, rows, width), BF16),
                dma(()),
                dma((n_doc,)),
                dma((n_z,)),
                dma((n_doc, 2)),
                dma((n_doc,)),
                dma(()),
                dma((n_z,)),
                dma((n_doc,)),
                dma((n_z,)),
                dma((n_doc, 2)),
                dma(()),
                dma(()),
                dma((n_z,)),
            ],
            compiler_params=pltpu.CompilerParams(
                collective_id=0, has_side_effects=True, vmem_limit_bytes=limit
            ),
        )(doc_embed, classifier, centroids, shortlist, positives.T)
        return settle(*outs)

    in_specs = (
        P(("doc", "label"), None),
        P("label", None),
        P("doc", None),
        P(("doc", "label"), None),
        P(("doc", "label"), None),
    )
    out_specs = (P("label", None), P("doc", None), P(("doc", "label"), None))
    return jax.shard_map(body, mesh=mesh, in_specs=in_specs, out_specs=out_specs, check_vma=False)
```

time: 40.4 us -> 30 us (0.74)
  local copies, waits for them, and re-layouts: 5.29 us -> 0 us
  Pallas kernels: 34.2 us -> 29.2 us
    pallas_call x1, Pallas kernels: 34.2 us -> 28 us  [body(): pl.pallas_call(functools.partial(kernel, n_doc, n_label, positives.shape[...]
    unnamed x8 -> x0, local copies, waits for them, and re-layouts: 5.29 us -> none
    pallas_call x0 -> x1, Pallas kernels: none -> 1.18 us  [settle(): pl.pallas_call(functools.partial(settle_kernel, n), out_shape=tuple((jax....]
where the time goes in v2:
time: 30 us; the launch traced here: 29.8 us
  Pallas kernels  29.2 us (97%)
  between operations  0.64 us (2%)
    pallas_call x1, Pallas kernels, body(): pl.pallas_call(functools.partial(kernel, n_doc, n_label, positives.shape[...  28 us
    pallas_call x1, Pallas kernels, settle(): pl.pallas_call(functools.partial(settle_kernel, n), out_shape=tuple((jax....  1.18 us

profile of v2, /device:TPU:0, one launch (start us, length us, event | category | flops | bytes accessed | tf_op | source)
XLA Modules:
  0.0 29.8 jit_solution(15850901550174050005)
XLA Ops:
  0.6 28.0 %shard_map.76 = (bf16[1024,768]{1,0:T(8,128)(2,1)S(1)}, f32[16,768]{1,0:T(8,128)S(1)}, bf16[32,768]{1,0:T(8,128)(2,1)S(1)}) custom-call(bf16[32,768]{1,0:T(8,128)(2,1)} %doc_ref.1, bf16[1024,768]{1,0:T(8,128)(2,1)} %cls_hbm.1, bf16[16,768]{1,0:T(8,128)(2,1)} %cent_ref.1, s32[32,32]{1,0:T(8,128)} %short_ref.1, s32[4,32]{1,0:T(4,128)} %bitcast.1), custom_call_target="tpu_custom_call" | custom-call | tf_op jit(solution)/shard_map/pallas_call | solution.py:262
  28.6 1.2 %shard_map.77 = (bf16[1024,768]{1,0:T(8,128)(2,1)}, f32[16,768]{1,0:T(8,128)}, bf16[32,768]{1,0:T(8,128)(2,1)}) custom-call(bf16[1024,768]{1,0:T(8,128)(2,1)S(1)} %get-tuple-element.6.refs_0_, f32[16,768]{1,0:T(8,128)S(1)} %get-tuple-element.7.refs_1_, bf16[32,768]{1,0:T(8,128)(2,1)S(1)} %get-tuple-element.8.refs_2_), custom_call_target="tpu_custom_call" | custom-call | tf_op jit(solution)/shard_map/pallas_call | solution.py:240
